TPU v7x, 512 devices: a whole 4x8x8 slice. The times are simulated.
512 devices in a mesh: gx: 32 (over y, x_lo, core), gy: 16 (over z, x_hi).
Axes of the slice: x: 4 (x_hi: 2, x_lo: 2; x = x_hi * 2 + x_lo), y: 8, z: 8, core: 2. Of those that a mesh axis runs over, the one named last changes fastest.
Arguments:
- west_in: float32 [2, 128, 1024, 128], P(None, 'gx', 'gy'), may hold values from -6 to 6
- south_in: float32 [2, 1024, 64, 128], P(None, 'gx', 'gy'), may hold values from -6 to 6
- region: int32 [1024, 1024], P('gx', 'gy'), may hold values from 0 to 7
- pml_layers: int32 [4, 32, 16], P(None, 'gx', 'gy'), may hold values from 0 to 8
- vel_table: float32 [8, 128], replicated, may hold values from 0.3 to 3
- src_slot: int32 [32, 16], P('gx', 'gy'), may hold values from 0 to 48
- src_cell: int32 [32, 16], P('gx', 'gy'), may hold values from 0 to 262143
- src_amp: float32 [2, 49], replicated, may hold values from -16 to 16
- wave_sq: float32 [], replicated, may hold values from 0.5 to 2
Outputs:
- fields: bfloat16 [3, 2, 1024, 1024, 128], P(None, None, 'gx', 'gy')
All inputs are finite; a program needn't handle non-finite values.
Results may differ from a plain program's by a relative error of at most 0.001.
Values sent between devices are 32-bit elements; how exact they have to be, the bound alone decides.
No kernel may reach another device: no remote copies, remote signals or barrier semaphores. Data moves between devices by JAX's collectives and lax.ppermute only.
A program may use at most 64 MiB of HBM per device.

v0:
```python
import functools

import jax
import jax.numpy as jnp
import ml_dtypes
import numpy as np
from jax import lax
from jax.experimental import pallas as pl
from jax.experimental.pallas import tpu as pltpu
from jax.sharding import PartitionSpec as P

DEPTH = 4
TICKS = 3
SUB = 8
GROUP = 4
DAMPING = 0.25
PEAK = 4.0
BASE = 6.0
F32 = jnp.float32
BF16 = jnp.bfloat16


def shift(array, axis):
    peers = lax.axis_size(axis)
    return lax.ppermute(array, axis, [(i, i + 1) for i in range(peers - 1)])


def basis(n):
    k = np.arange(1, n + 1, dtype=np.float64)
    table = np.sqrt(2.0 / (n + 1)) * np.sin(np.pi * np.outer(k, k) / (n + 1))
    return table, 2.0 - 2.0 * np.cos(np.pi * k / (n + 1))


def halves(table):
    high = table.astype(ml_dtypes.bfloat16)
    low = (table - high.astype(np.float64)).astype(ml_dtypes.bfloat16)
    return high, low


def stacked(table):
    high, low = halves(table)
    return np.block([[high, high], [low, np.zeros_like(low)]])


def constants(sx, sy, sz):
    bx, ex = basis(sx)
    by, ey = basis(sy)
    bz, ez = basis(sz)
    zh, zl = halves(bz)
    half = sx // 2
    eye = np.eye(SUB)
    narrow = {
        "z": np.block([[zh, zl], [zh, zl]]),
        "even": stacked(np.kron(bx[:half, 0::2], eye)),
        "odd": stacked(np.kron(bx[:half, 1::2], eye)),
        "y": stacked(by),
        "south": stacked(np.kron(bx, np.eye(DEPTH))),
        "west": np.concatenate(halves(np.kron(bx[order(sx), :DEPTH], eye)), axis=1),
    }
    wide = {
        "eigen": ey[:, None] + ez[None, :],
        "bx": bx,
        "by": by,
        "bz": bz,
        "reach": np.repeat(by[:, :DEPTH].T.reshape(DEPTH * sy, 1), sz, axis=1),
    }
    return pack(narrow, ml_dtypes.bfloat16), pack(wide, np.float32)


def order(sx):
    return list(range(0, sx, 2)) + list(range(1, sx, 2))


def pack(tables, dtype):
    width = max(t.shape[1] for t in tables.values())
    rows, places, at = [], {}, 0
    for name, t in tables.items():
        places[name] = (at, t.shape)
        rows.append(np.pad(t.astype(np.float64), ((0, 0), (0, width - t.shape[1]))))
        at += t.shape[0]
    return np.concatenate(rows).astype(dtype), places


def split(values):
    high = values.astype(BF16)
    low = (values - high.astype(F32)).astype(BF16)
    return high, low


def dot(a, b):
    return jnp.dot(a, b, preferred_element_type=F32)


def along_z(rows, z_table):
    high, low = split(rows)
    both = dot(jnp.concatenate([high, low], axis=1), z_table)
    size_z = rows.shape[1]
    return both[:, :size_z] + both[:, size_z:]


def from_left(table, rows):
    high, low = split(rows)
    both = dot(table, jnp.concatenate([high, low], axis=0))
    n = both.shape[0] // 2
    return both[:n] + both[n:]


def ramp(layers, distance):
    portion = jnp.maximum(layers - distance, 0.0) / jnp.maximum(layers, 1.0)
    return portion * portion


def point_rows(sizes, values, slot, cell, amp, wave, aux):
    sx, sy, sz = sizes
    bits = [size.bit_length() - 1 for size in sizes]
    number = cell[...]
    cell_x = lax.shift_right_logical(number, bits[1] + bits[2])
    cell_y = lax.shift_right_logical(number, bits[2]) & (sy - 1)
    cell_z = number & (sz - 1)

    def column(name, size, where):
        lane = lax.broadcasted_iota(jnp.int32, (size, sz), 1)
        return jnp.sum(jnp.where(lane == where, values(name, 0, size), 0.0), axis=1, keepdims=True)

    aux[:sy] = jnp.broadcast_to(column("by", sy, cell_y), (sy, sz))
    row = lax.broadcasted_iota(jnp.int32, (sz, sz), 0)
    bz_row = jnp.sum(jnp.where(row == cell_z, values("bz", 0, sz), 0.0), axis=0, keepdims=True)
    aux[sy : sy + sx] = column("bx", sx, cell_x) * bz_row
    first = lax.axis_size("gx") + lax.axis_size("gy") - 2 - lax.axis_index("gx") - lax.axis_index("gy")
    lane = lax.broadcasted_iota(jnp.int32, amp.shape, 1)
    at = sy + sx
    for tick in range(TICKS):
        strength = jnp.sum(jnp.where(lane == first + tick, amp[...], 0.0), axis=1, keepdims=True)
        strength = jnp.where(slot[...] == first + tick, strength, 0.0)
        aux[at + 2 * tick : at + 2 * tick + 2] = jnp.broadcast_to(strength, (2, sz))
    at += 2 * TICKS
    aux[at : at + 1] = jnp.broadcast_to(wave[...], (1, sz))


def aux_rows(sizes):
    sx, sy, _ = sizes
    return -(-(sx + sy + 2 * TICKS + 1) // SUB) * SUB


def tick_kernel(tick, sizes, places, *refs):
    sx, sy, sz = sizes
    refs = list(refs)
    take = lambda n: [refs.pop(0) for _ in range(n)]
    last = tick + 1 == TICKS
    fields = []
    if tick == 0:
        fetched = take(11)
        east, north, field, narrow, wide, aux, gain_re, gain_im = take(8)
    else:
        narrow, wide, aux, gain_re, gain_im, west, south = take(7)
        if last:
            fields = take(TICKS - 1)
            (out,) = take(1)
        else:
            east, north, field = take(3)
    west_hat, south_hat, grid = take(3)
    fetches = []
    if tick == 0:
        west, south, region, vel, layers, slot, cell, amp, wave = take(9)
        (fetch_sems,) = take(1)
        for i, target in enumerate([narrow, wide, west, south, region, vel, layers, slot, cell, amp, wave]):
            copy = pltpu.make_async_copy(fetched[i], target, fetch_sems.at[i])
            copy.start()
            fetches.append(copy)
        for copy in fetches:
            copy.wait()
    copies = []
    if last:
        field, sems = take(2)
        for i, earlier in enumerate(fields):
            copy = pltpu.make_async_copy(earlier, out.at[i], sems.at[i])
            copy.start()
            copies.append(copy)

    def table(name):
        at, shape = places[0][name]
        return narrow[at : at + shape[0], : shape[1]]

    def values(name, start, size):
        at, shape = places[1][name]
        return wide[at + start : at + start + size, :]

    if tick == 0:
        point_rows(sizes, values, slot, cell, amp, wave, aux)
    n_blocks = sy // SUB
    half = sx // 2
    at = sy + sx + 2 * TICKS
    w2 = aux[at : at + 1]
    eigen_x = [float(v) for v in basis(sx)[1].astype(np.float32)]

    zt = table("z")
    west_rows = along_z(west[...].reshape(2 * DEPTH * sy, sz), zt).reshape(2, DEPTH, sy, sz)
    for d in range(DEPTH):
        west_hat[d] = from_left(table("y"), jnp.concatenate([west_rows[0, d], west_rows[1, d]], axis=1))
    south_rows = along_z(south[...].reshape(2 * DEPTH * sx, sz), zt).reshape(2, DEPTH * sx, sz)
    n_south = DEPTH * sx
    south_hat[:n_south] = from_left(table("south"), jnp.concatenate([south_rows[0], south_rows[1]], axis=1))
    for c in range(2):
        row = sy + sx + 2 * tick + c
        south_hat[n_south:, c * sz : (c + 1) * sz] = aux[sy : sy + sx] * aux[row : row + 1]
    damping = jnp.broadcast_to(-DAMPING * w2, (SUB, sz))
    damping_square = damping * damping

    for j in range(n_blocks):
        here = slice(j * SUB, (j + 1) * SUB)
        high, low = split(west_hat[:, here, :].reshape(DEPTH * SUB, 2 * sz))
        west_table = table("west")
        n = DEPTH * SUB
        coeffs = dot(
            jnp.concatenate([west_table[:, :n], west_table[:, :n], west_table[:, n:]], axis=1),
            jnp.concatenate([high, low, high], axis=0),
        )
        base = values("eigen", j * SUB, SUB) - w2
        reach = [values("reach", d * sy + j * SUB, SUB) for d in range(DEPTH)] + [aux[here]]
        new_re = []
        new_im = []
        for i, k in enumerate(order(sx)):
            line = slice(i * SUB, (i + 1) * SUB)
            c_re = coeffs[line, :sz]
            c_im = coeffs[line, sz:]
            for d in range(DEPTH + 1):
                row = k * DEPTH + d if d < DEPTH else n_south + k
                row = slice(row, row + 1)
                c_re += reach[d] * south_hat[row, :sz]
                c_im += reach[d] * south_hat[row, sz:]
            shifted = base + eigen_x[k]
            size = shifted * shifted + damping_square
            inverse = pl.reciprocal(size, approx=True)
            inverse = inverse * (2.0 - size * inverse)
            p = shifted * inverse
            q = damping * inverse
            new_re.append(c_re * p + c_im * q)
            new_im.append(c_im * p - c_re * q)
        lines = along_z(jnp.concatenate(new_re + new_im, axis=0), zt)
        n = half * SUB
        e = from_left(table("even"), jnp.concatenate([lines[:n], lines[2 * n : 3 * n]], axis=1))
        o = from_left(table("odd"), jnp.concatenate([lines[n : 2 * n], lines[3 * n :]], axis=1))
        grid[:half, here, :] = (e + o).reshape(half, SUB, 2 * sz)
        difference = e - o
        for x in range(half):
            grid[sx - 1 - x, here, :] = difference[x * SUB : (x + 1) * SUB]

    if tick == 0:
        y_pos = lax.broadcasted_iota(jnp.int32, (sy, 1), 0).astype(F32)
        as_f = lambda i: layers[:, i : i + 1].astype(F32)
        sigma_y = ramp(as_f(2), y_pos) + ramp(as_f(3), sy - 1.0 - y_pos)
        labels = region[...].astype(F32).T
        count = vel.shape[0]
        contrast = vel[...] - w2
        vh, vl = split(contrast)
        vel_rows = jnp.concatenate([vh, vl], axis=0)
        label_lane = (lax.broadcasted_iota(jnp.int32, (sy, 2 * count), 1) % count).astype(F32)

    for x in range(sx):
        raw = from_left(table("y"), grid[x])
        raw_re = raw[:, :sz]
        raw_im = raw[:, sz:]
        if tick == 0:
            hot = (labels[:, x : x + 1] == label_lane).astype(BF16)
            c = dot(hot, vel_rows)
            x_pos = jnp.full((1, 1), float(x), F32)
            sigma_x = ramp(as_f(0), x_pos) + ramp(as_f(1), sx - 1.0 - x_pos)
            sigma = PEAK * (sigma_x + sigma_y)
            inverse = 1.0 / (BASE * BASE + sigma * sigma)
            g_re = 1.0 + c * (BASE * inverse)
            g_im = -c * (sigma * inverse)
            gain_re[x] = g_re
            gain_im[x] = g_im
        else:
            g_re = gain_re[x]
            g_im = gain_im[x]
        f_re = raw_re * g_re - raw_im * g_im
        f_im = raw_im * g_re + raw_re * g_im
        field[0, x] = f_re.astype(BF16)
        field[1, x] = f_im.astype(BF16)
        if not last:
            if x >= sx - DEPTH:
                east[0, x - (sx - DEPTH)] = f_re
                east[1, x - (sx - DEPTH)] = f_im
            north[0, DEPTH * x : DEPTH * (x + 1), :] = f_re[sy - DEPTH :]
            north[1, DEPTH * x : DEPTH * (x + 1), :] = f_im[sy - DEPTH :]
        elif x % GROUP == GROUP - 1:
            span = pl.ds(x - GROUP + 1, GROUP)
            copy = pltpu.make_async_copy(field.at[:, span], out.at[tick, :, span], sems.at[len(copies)])
            copy.start()
            copies.append(copy)
    for copy in copies:
        copy.wait()


def run_tick(tick, sizes, places, args):
    sx, sy, sz = sizes
    vm = pl.BlockSpec(memory_space=pltpu.VMEM)
    last = tick + 1 == TICKS
    whole = jax.ShapeDtypeStruct((2, sx, sy, sz), BF16)
    scratch = [
        pltpu.VMEM((DEPTH, sy, 2 * sz), F32),
        pltpu.VMEM((sx * (DEPTH + 1), 2 * sz), F32),
        pltpu.VMEM((sx, sy, 2 * sz), F32),
    ]
    in_specs = [vm] * len(args)
    if last:
        out_shape = [jax.ShapeDtypeStruct((TICKS, *whole.shape), BF16)]
        out_specs = [pl.BlockSpec(memory_space=pl.ANY)]
        scratch += [pltpu.VMEM(whole.shape, BF16), pltpu.SemaphoreType.DMA((TICKS - 1 + sx // GROUP,))]
    else:
        out_shape = [
            jax.ShapeDtypeStruct((2, DEPTH, sy, sz), F32),
            jax.ShapeDtypeStruct((2, sx * DEPTH, sz), F32),
            whole,
        ]
        if tick == 0:
            in_specs = [pl.BlockSpec(memory_space=pltpu.HBM)] * len(args)
            narrow, wide = args[:2]
            args = [pltpu.with_memory_space_constraint(a, pltpu.HBM) if a.size > 1 else a for a in args]
            out_shape += [jax.ShapeDtypeStruct(t.shape, t.dtype) for t in (narrow, wide)]
            out_shape += [jax.ShapeDtypeStruct((aux_rows(sizes), sz), F32)]
            out_shape += [jax.ShapeDtypeStruct((sx, sy, sz), F32)] * 2
            scratch += [pltpu.VMEM(a.shape, a.dtype) for a in args[2:]] + [pltpu.SemaphoreType.DMA((len(args),))]
        out_specs = [vm] * len(out_shape)
    return pl.pallas_call(
        functools.partial(tick_kernel, tick, sizes, places),
        out_shape=out_shape,
        in_specs=in_specs,
        out_specs=out_specs,
        scratch_shapes=scratch,
        compiler_params=pltpu.CompilerParams(vmem_limit_bytes=24 * 1024 * 1024),
        name=f"tick{tick}",
    )(*args)


def local(west_in, south_in, region, pml_layers, vel_table, src_slot, src_cell, src_amp, wave_sq):
    sx, sy = region.shape
    sz = vel_table.shape[1]
    sizes = (sx, sy, sz)
    (narrow, narrow_at), (wide, wide_at) = constants(sx, sy, sz)
    places = (narrow_at, wide_at)
    args = [jnp.asarray(narrow), jnp.asarray(wide), west_in, south_in.reshape(2, sx * DEPTH, sz), region, vel_table]
    args += [pml_layers.reshape(1, 4), src_slot, src_cell, src_amp, wave_sq.reshape(1, 1)]
    east, north, field, *kept = run_tick(0, sizes, places, args)
    fields = [field]
    for tick in range(1, TICKS):
        west = shift(east, "gx")
        south = shift(north, "gy")
        if tick + 1 < TICKS:
            east, north, field = run_tick(tick, sizes, places, [*kept, west, south])
            fields.append(field)
    (out,) = run_tick(TICKS - 1, sizes, places, [*kept, west, south, *fields])
    return out


def solution(mesh):
    in_specs = (
        P(None, "gx", "gy", None),
        P(None, "gx", "gy", None),
        P("gx", "gy"),
        P(None, "gx", "gy"),
        P(),
        P("gx", "gy"),
        P("gx", "gy"),
        P(),
        P(),
    )
    out_specs = P(None, None, "gx", "gy", None)
    return jax.shard_map(local, mesh=mesh, in_specs=in_specs, out_specs=out_specs, check_vma=False)
```

profile of v0, /device:TPU:283, one launch (start us, length us, event | category | flops | bytes accessed | tf_op | source)
XLA Modules:
  0.0 48.0 jit_solution(12401426958511078534)
XLA Ops:
  1.9 6.9 %tick0.1 = (f32[2,4,64,128]{3,2,1,0:T(8,128)S(1)}, f32[2,128,128]{2,1,0:T(8,128)S(1)}, bf16[2,32,64,128]{3,2,1,0:T(8,128)(2,1)S(1)}, bf16[1408,256]{1,0:T(8,128)...) custom-call(bf16[1408,256]{1,0:T(8,128)(2,1)} %constant.4.clone.refs, ...), custom_call_target="tpu_custom_call" | custom-call | tf_op jit(solution)/shard_map/tick0/pallas_call | solution.py:326
  8.9 4.9 %collective-permute-start = (f32[2,4,64,128]{3,2,1,0:T(8,128)S(1)}, f32[2,4,64,128]{3,2,1,0:T(8,128)S(1)}, u32[]{:S(2)}, u32[]{:S(2)}) collective-permute-start(f32[2,4,64,128]{3,2,1,0:T(8,128)S(1)} %get-tuple-element.21), channel_id=1, source_target_pairs={{0,16},{16,32},{32,48},{48,64},{64,80},{80,96},{96,112},{112,128},... | collective-permute-start | bytes 786440 | tf_op jit(solution)/shard_map/ppermute | solution.py:25
  13.8 4.1 %collective-permute-start.1 = (f32[2,128,128]{2,1,0:T(8,128)S(1)}, f32[2,128,128]{2,1,0:T(8,128)S(1)}, u32[]{:S(2)}, u32[]{:S(2)}) collective-permute-start(f32[2,128,128]{2,1,0:T(8,128)S(1)} %get-tuple-element.22), channel_id=1, source_target_pairs={{0,1},{1,2},{2,3},{3,4},{4,5},{5,6},{6,7},{7,8},{8,9},{9,10},{10,1... | collective-permute-start | bytes 393224 | tf_op jit(solution)/shard_map/ppermute | solution.py:25
  17.9 5.3 %collective-permute-done.1.refs_6_ = f32[2,128,128]{2,1,0:T(8,128)S(1)} collective-permute-done((f32[2,128,128]{2,1,0:T(8,128)S(1)}, f32[2,128,128]{2,1,0:T(8,128)S(1)}, u32[]{:S(2)}, u32[]{:S(2)}) %collective-permute-start.1) | collective-permute-done | bytes 131104 | tf_op jit(solution)/shard_map/ppermute | solution.py:25
  23.2 0.0 collective-permute-done.refs_5_
  23.2 5.2 %tick1.1 = (f32[2,4,64,128]{3,2,1,0:T(8,128)S(1)}, f32[2,128,128]{2,1,0:T(8,128)S(1)}, bf16[2,32,64,128]{3,2,1,0:T(8,128)(2,1)S(1)}) custom-call(bf16[1408,256]{1,0:T(8,128)(2,1)S(1)} %get-tuple-element.16.refs_0_, f32[544,128]{1,0:T(8,128)S(1)} %get-tuple-element.17.refs_1_, f32[104,128]{1,0:T(8,128)S(1)} %get-tuple-element.18.refs_2_, ...), custom_call_target="tpu_custom_call" | custom-call | tf_op jit(solution)/shard_map/tick1/pallas_call | solution.py:326
  28.4 3.9 %collective-permute-start.2 = (f32[2,4,64,128]{3,2,1,0:T(8,128)S(1)}, f32[2,4,64,128]{3,2,1,0:T(8,128)S(1)}, u32[]{:S(2)}, u32[]{:S(2)}) collective-permute-start(f32[2,4,64,128]{3,2,1,0:T(8,128)S(1)} %get-tuple-element.23), channel_id=1, source_target_pairs={{0,16},{16,32},{32,48},{48,64},{64,80},{80,96},{96,112},{112,128},... | collective-permute-start | bytes 786440 | tf_op jit(solution)/shard_map/ppermute | solution.py:25
  32.2 2.4 %collective-permute-start.3 = (f32[2,128,128]{2,1,0:T(8,128)S(1)}, f32[2,128,128]{2,1,0:T(8,128)S(1)}, u32[]{:S(2)}, u32[]{:S(2)}) collective-permute-start(f32[2,128,128]{2,1,0:T(8,128)S(1)} %get-tuple-element.24), channel_id=1, source_target_pairs={{0,1},{1,2},{2,3},{3,4},{4,5},{5,6},{6,7},{7,8},{8,9},{9,10},{10,1... | collective-permute-start | bytes 393224 | tf_op jit(solution)/shard_map/ppermute | solution.py:25
  34.6 7.3 %collective-permute-done.3.refs_6_ = f32[2,128,128]{2,1,0:T(8,128)S(1)} collective-permute-done((f32[2,128,128]{2,1,0:T(8,128)S(1)}, f32[2,128,128]{2,1,0:T(8,128)S(1)}, u32[]{:S(2)}, u32[]{:S(2)}) %collective-permute-start.3) | collective-permute-done | bytes 131104 | tf_op jit(solution)/shard_map/ppermute | solution.py:25
  42.0 0.0 collective-permute-done.2.refs_5_
  42.0 5.9 %tick2.1 = bf16[3,2,32,64,128]{4,3,2,1,0:T(8,128)(2,1)} custom-call(bf16[1408,256]{1,0:T(8,128)(2,1)S(1)} %get-tuple-element.16.refs_0_, f32[544,128]{1,0:T(8,128)S(1)} %get-tuple-element.17.refs_1_, f32[104,128]{1,0:T(8,128)S(1)} %get-tuple-element.18.refs_2_, f32[32,64,128]{2,1,0:T(8,128)S(1)} %get-tuple-element.19.refs_3_, ...), custom_call_target="tpu_custom_call" | custom-call | tf_op jit(solution)/shard_map/tick2/pallas_call | solution.py:326
Async XLA Ops:
  8.9 14.3 %collective-permute-start = (f32[2,4,64,128]{3,2,1,0:T(8,128)S(1)}, f32[2,4,64,128]{3,2,1,0:T(8,128)S(1)}, u32[]{:S(2)}, u32[]{:S(2)}) collective-permute-start(f32[2,4,64,128]{3,2,1,0:T(8,128)S(1)} %get-tuple-element.21), channel_id=1, source_target_pairs={{0,16},{16,32},{32,48},{48,64},{64,80},{80,96},{96,112},{112,128},... | collective-permute-start | bytes 786440 | tf_op jit(solution)/shard_map/ppermute | solution.py:25
  13.8 9.3 %collective-permute-start.1 = (f32[2,128,128]{2,1,0:T(8,128)S(1)}, f32[2,128,128]{2,1,0:T(8,128)S(1)}, u32[]{:S(2)}, u32[]{:S(2)}) collective-permute-start(f32[2,128,128]{2,1,0:T(8,128)S(1)} %get-tuple-element.22), channel_id=1, source_target_pairs={{0,1},{1,2},{2,3},{3,4},{4,5},{5,6},{6,7},{7,8},{8,9},{9,10},{10,1... | collective-permute-start | bytes 393224 | tf_op jit(solution)/shard_map/ppermute | solution.py:25
  28.4 13.6 %collective-permute-start.2 = (f32[2,4,64,128]{3,2,1,0:T(8,128)S(1)}, f32[2,4,64,128]{3,2,1,0:T(8,128)S(1)}, u32[]{:S(2)}, u32[]{:S(2)}) collective-permute-start(f32[2,4,64,128]{3,2,1,0:T(8,128)S(1)} %get-tuple-element.23), channel_id=1, source_target_pairs={{0,16},{16,32},{32,48},{48,64},{64,80},{80,96},{96,112},{112,128},... | collective-permute-start | bytes 786440 | tf_op jit(solution)/shard_map/ppermute | solution.py:25
  32.2 9.7 %collective-permute-start.3 = (f32[2,128,128]{2,1,0:T(8,128)S(1)}, f32[2,128,128]{2,1,0:T(8,128)S(1)}, u32[]{:S(2)}, u32[]{:S(2)}) collective-permute-start(f32[2,128,128]{2,1,0:T(8,128)S(1)} %get-tuple-element.24), channel_id=1, source_target_pairs={{0,1},{1,2},{2,3},{3,4},{4,5},{5,6},{6,7},{7,8},{8,9},{9,10},{10,1... | collective-permute-start | bytes 393224 | tf_op jit(solution)/shard_map/ppermute | solution.py:25
where the time goes:
time: 48.3 us; the launch traced here: 48 us
  Pallas kernels  18 us (37%)
  starting transfers between devices  15.3 us (32%)
  waiting for transfers between devices  12.6 us (26%)
  between operations  2.15 us (4%)
    pallas_call x3, Pallas kernels, run_tick(): pl.pallas_call(functools.partial(tick_kernel, tick, sizes, places), out_s...  18 us
    ppermute x4, starting transfers between devices, shift(): return lax.ppermute(array, axis, [(i, i + 1) for i in range(peers - 1)])  15.3 us
    ppermute x4, waiting for transfers between devices, shift(): return lax.ppermute(array, axis, [(i, i + 1) for i in range(peers - 1)])  12.6 us
  transfers between devices with their start and end apart: 4, of which 2 were waited for; matrix products, arithmetic and copies ran while one was open for 0% of the time, Pallas kernels for 0%

commit v1 on v0

v1 whole, which is shorter than its diff:
```python
import functools

import jax
import jax.numpy as jnp
import ml_dtypes
import numpy as np
from jax import lax
from jax.experimental import pallas as pl
from jax.experimental.pallas import tpu as pltpu
from jax.sharding import PartitionSpec as P

DEPTH = 4
TICKS = 3
SUB = 8
GROUP = 4
DAMPING = 0.25
PEAK = 4.0
BASE = 6.0
F32 = jnp.float32
BF16 = jnp.bfloat16


def shift(array, axis):
    peers = lax.axis_size(axis)
    return lax.ppermute(array, axis, [(i, i + 1) for i in range(peers - 1)])


def basis(n):
    k = np.arange(1, n + 1, dtype=np.float64)
    table = np.sqrt(2.0 / (n + 1)) * np.sin(np.pi * np.outer(k, k) / (n + 1))
    return table, 2.0 - 2.0 * np.cos(np.pi * k / (n + 1))


def halves(table):
    high = table.astype(ml_dtypes.bfloat16)
    low = (table - high.astype(np.float64)).astype(ml_dtypes.bfloat16)
    return high, low


def stacked(table):
    high, low = halves(table)
    return np.block([[high, high], [low, np.zeros_like(low)]])


def constants(sx, sy, sz):
    bx, ex = basis(sx)
    by, ey = basis(sy)
    bz, ez = basis(sz)
    zh, zl = halves(bz)
    half = sx // 2
    eye = np.eye(SUB)
    narrow = {
        "z": np.block([[zh, zl], [zh, zl]]),
        "even": stacked(np.kron(bx[:half, 0::2], eye)),
        "odd": stacked(np.kron(bx[:half, 1::2], eye)),
        "y": stacked(by),
        "south": stacked(np.kron(bx, np.eye(DEPTH))),
        "west": np.concatenate(halves(np.kron(bx[order(sx), :DEPTH], eye)), axis=1),
    }
    wide = {
        "eigen": ey[:, None] + ez[None, :],
        "bx": bx,
        "by": by,
        "bz": bz,
        "reach": np.repeat(by[:, :DEPTH].T.reshape(DEPTH * sy, 1), sz, axis=1),
    }
    east = halves(np.kron(bx[sx - DEPTH :, order(sx)], eye))
    north = []
    for j in range(sy // SUB):
        north += halves(np.kron(np.eye(sx)[:, order(sx)], by[sy - DEPTH :, j * SUB : (j + 1) * SUB]))
    traces = np.concatenate([*east, *north])
    return pack(narrow, ml_dtypes.bfloat16), pack(wide, np.float32), traces


def order(sx):
    return list(range(0, sx, 2)) + list(range(1, sx, 2))


def pack(tables, dtype):
    width = max(t.shape[1] for t in tables.values())
    rows, places, at = [], {}, 0
    for name, t in tables.items():
        places[name] = (at, t.shape)
        rows.append(np.pad(t.astype(np.float64), ((0, 0), (0, width - t.shape[1]))))
        at += t.shape[0]
    return np.concatenate(rows).astype(dtype), places


def split(values):
    high = values.astype(BF16)
    low = (values - high.astype(F32)).astype(BF16)
    return high, low


def dot(a, b):
    return jnp.dot(a, b, preferred_element_type=F32)


def along_z(rows, z_table):
    high, low = split(rows)
    both = dot(jnp.concatenate([high, low], axis=1), z_table)
    size_z = rows.shape[1]
    return both[:, :size_z] + both[:, size_z:]


def from_left(table, rows):
    high, low = split(rows)
    both = dot(table, jnp.concatenate([high, low], axis=0))
    n = both.shape[0] // 2
    return both[:n] + both[n:]


def ramp(layers, distance):
    portion = jnp.maximum(layers - distance, 0.0) / jnp.maximum(layers, 1.0)
    return portion * portion


def point_rows(sizes, values, slot, cell, amp, wave, aux):
    sx, sy, sz = sizes
    bits = [size.bit_length() - 1 for size in sizes]
    number = cell[...]
    cell_x = lax.shift_right_logical(number, bits[1] + bits[2])
    cell_y = lax.shift_right_logical(number, bits[2]) & (sy - 1)
    cell_z = number & (sz - 1)

    def column(name, size, where):
        lane = lax.broadcasted_iota(jnp.int32, (size, sz), 1)
        return jnp.sum(jnp.where(lane == where, values(name, 0, size), 0.0), axis=1, keepdims=True)

    aux[:sy] = jnp.broadcast_to(column("by", sy, cell_y), (sy, sz))
    row = lax.broadcasted_iota(jnp.int32, (sz, sz), 0)
    bz_row = jnp.sum(jnp.where(row == cell_z, values("bz", 0, sz), 0.0), axis=0, keepdims=True)
    aux[sy : sy + sx] = column("bx", sx, cell_x) * bz_row
    first = lax.axis_size("gx") + lax.axis_size("gy") - 2 - lax.axis_index("gx") - lax.axis_index("gy")
    lane = lax.broadcasted_iota(jnp.int32, amp.shape, 1)
    at = sy + sx
    for tick in range(TICKS):
        strength = jnp.sum(jnp.where(lane == first + tick, amp[...], 0.0), axis=1, keepdims=True)
        strength = jnp.where(slot[...] == first + tick, strength, 0.0)
        aux[at + 2 * tick : at + 2 * tick + 2] = jnp.broadcast_to(strength, (2, sz))
    at += 2 * TICKS
    aux[at : at + 1] = jnp.broadcast_to(wave[...], (1, sz))


def aux_rows(sizes):
    sx, sy, _ = sizes
    return -(-(sx + sy + 2 * TICKS + 1) // SUB) * SUB


def table_of(narrow, places):
    def table(name):
        at, shape = places[name]
        return narrow[at : at + shape[0], : shape[1]]

    return table


def values_of(wide, places):
    def values(name, start, size):
        at, shape = places[name]
        return wide[at + start : at + start + size, :]

    return values


def wave_row(sizes, aux):
    at = sizes[0] + sizes[1] + 2 * TICKS
    return aux[at : at + 1]


def spread_west(sizes, table, west, west_hat):
    sx, sy, sz = sizes
    rows = along_z(west[...].reshape(2 * DEPTH * sy, sz), table("z")).reshape(2, DEPTH, sy, sz)
    for d in range(DEPTH):
        west_hat[d] = from_left(table("y"), jnp.concatenate([rows[0, d], rows[1, d]], axis=1))
    n = DEPTH * SUB
    west_table = table("west")
    left = jnp.concatenate([west_table[:, :n], west_table[:, :n], west_table[:, n:]], axis=1)
    blocks = []
    for j in range(sy // SUB):
        high, low = split(west_hat[:, j * SUB : (j + 1) * SUB, :].reshape(n, 2 * sz))
        blocks.append(dot(left, jnp.concatenate([high, low, high], axis=0)))
    return blocks


def transform_south(sizes, table, south, south_hat):
    sx, _, sz = sizes
    n = DEPTH * sx
    rows = along_z(south[...].reshape(2 * n, sz), table("z")).reshape(2, n, sz)
    south_hat[:n] = from_left(table("south"), jnp.concatenate([rows[0], rows[1]], axis=1))


def place_point(tick, sizes, aux, south_hat):
    sx, sy, sz = sizes
    for c in range(2):
        row = sy + sx + 2 * tick + c
        south_hat[DEPTH * sx :, c * sz : (c + 1) * sz] = aux[sy : sy + sx] * aux[row : row + 1]


def spectrum_block(j, sizes, coeffs, values, aux, south_hat):
    sx, sy, sz = sizes
    here = slice(j * SUB, (j + 1) * SUB)
    eigen_x = [float(v) for v in basis(sx)[1].astype(np.float32)]
    w2 = wave_row(sizes, aux)
    damping = jnp.broadcast_to(-DAMPING * w2, (SUB, sz))
    damping_square = damping * damping
    base = values("eigen", j * SUB, SUB) - w2
    reach = [values("reach", d * sy + j * SUB, SUB) for d in range(DEPTH)] + [aux[here]]
    new_re = []
    new_im = []
    for i, k in enumerate(order(sx)):
        line = slice(i * SUB, (i + 1) * SUB)
        c_re = coeffs[line, :sz]
        c_im = coeffs[line, sz:]
        for d in range(DEPTH + 1):
            row = k * DEPTH + d if d < DEPTH else sx * DEPTH + k
            row = slice(row, row + 1)
            c_re += reach[d] * south_hat[row, :sz]
            c_im += reach[d] * south_hat[row, sz:]
        shifted = base + eigen_x[k]
        size = shifted * shifted + damping_square
        inverse = pl.reciprocal(size, approx=True)
        inverse = inverse * (2.0 - size * inverse)
        p = shifted * inverse
        q = damping * inverse
        new_re.append(c_re * p + c_im * q)
        new_im.append(c_im * p - c_re * q)
    return jnp.concatenate(new_re, axis=0), jnp.concatenate(new_im, axis=0)


def invert_block(j, sizes, table, rows, grid):
    sx, _, sz = sizes
    half = sx // 2
    here = slice(j * SUB, (j + 1) * SUB)
    lines = along_z(rows, table("z"))
    n = half * SUB
    e = from_left(table("even"), jnp.concatenate([lines[:n], lines[2 * n : 3 * n]], axis=1))
    o = from_left(table("odd"), jnp.concatenate([lines[n : 2 * n], lines[3 * n :]], axis=1))
    grid[:half, here, :] = (e + o).reshape(half, SUB, 2 * sz)
    difference = e - o
    for x in range(half):
        grid[sx - 1 - x, here, :] = difference[x * SUB : (x + 1) * SUB]


def gains_of(sizes, layers, vel, w2):
    sx, sy, _ = sizes
    count = vel.shape[0]
    layer = [layers[:, i : i + 1].astype(F32) for i in range(4)]
    rows = jnp.concatenate(split(vel[...] - w2), axis=0)

    def gains(labels, x_pos, y_pos):
        n = labels.shape[0]
        lane = (lax.broadcasted_iota(jnp.int32, (n, 2 * count), 1) % count).astype(F32)
        contrast = dot((labels == lane).astype(BF16), rows)
        sigma = ramp(layer[0], x_pos) + ramp(layer[1], sx - 1.0 - x_pos)
        sigma = PEAK * (sigma + ramp(layer[2], y_pos) + ramp(layer[3], sy - 1.0 - y_pos))
        inverse = 1.0 / (BASE * BASE + sigma * sigma)
        return 1.0 + contrast * (BASE * inverse), -contrast * (sigma * inverse)

    return gains


def y_places(sizes):
    return lax.broadcasted_iota(jnp.int32, (sizes[1], 1), 0).astype(F32)


def correct(raw_re, raw_im, g_re, g_im):
    return raw_re * g_re - raw_im * g_im, raw_im * g_re + raw_re * g_im


def trace_gains(sizes, region, vel, layers, wave, gain_east, gain_north):
    sx, sy, _ = sizes
    n_north = DEPTH * sx
    gains = gains_of(sizes, layers, vel, wave[...])
    labels = region[...].astype(F32)
    columns = labels.T
    for d in range(DEPTH):
        x = sx - DEPTH + d
        g_re, g_im = gains(columns[:, x : x + 1], jnp.full((1, 1), float(x), F32), y_places(sizes))
        gain_east[0, d] = g_re
        gain_east[1, d] = g_im
    row = lax.broadcasted_iota(jnp.int32, (n_north, sx), 0)
    repeat = (row // DEPTH == lax.broadcasted_iota(jnp.int32, (n_north, sx), 1)).astype(BF16)
    spread = dot(repeat, labels.astype(BF16))
    row = lax.broadcasted_iota(jnp.int32, (n_north, sy), 0)
    lane = lax.broadcasted_iota(jnp.int32, (n_north, sy), 1)
    mine = jnp.sum(jnp.where(lane == sy - DEPTH + row % DEPTH, spread, 0.0), axis=1, keepdims=True)
    row = lax.broadcasted_iota(jnp.int32, (n_north, 1), 0)
    x_pos = (row // DEPTH).astype(F32)
    y_pos = (sy - DEPTH + row % DEPTH).astype(F32)
    g_re, g_im = gains(mine, x_pos, y_pos)
    gain_north[0] = g_re
    gain_north[1] = g_im


def traces_kernel(tick, sizes, places, *refs):
    sx, sy, sz = sizes
    refs = list(refs)
    take = lambda n: [refs.pop(0) for _ in range(n)]
    waits = []
    if tick == 0:
        fetched = take(12)
        fetched = fetched[4:8] + fetched[9:] + fetched[:4] + fetched[8:9]
        east, north, spectrum, narrow, wide, tall, aux, gain_east, gain_north, region, vel, layers = take(12)
    else:
        narrow, wide, tall, aux, gain_east, gain_north, from_west, south = take(8)
        east, north, spectrum = take(3)
    south_hat, east_hat = take(2)
    if tick == 0:
        west_hat, west, south, slot, cell, amp, wave = take(7)
        (fetch_sems,) = take(1)
        targets = [slot, cell, amp, wave, region, vel, layers, narrow, west, south, wide, tall]
        for i, target in enumerate(targets):
            copy = pltpu.make_async_copy(fetched[i], target, fetch_sems.at[i])
            copy.start()
            waits.append(copy)
        for copy in waits[:7]:
            copy.wait()
    table = table_of(narrow, places[0])
    values = values_of(wide, places[1])
    n_east = DEPTH * SUB
    n_north = DEPTH * sx
    if tick == 0:
        trace_gains(sizes, region, vel, layers, wave, gain_east, gain_north)
        for copy in waits[7:10]:
            copy.wait()
        starts = spread_west(sizes, table, west, west_hat)
    transform_south(sizes, table, south, south_hat)
    if tick == 0:
        for copy in waits[10:]:
            copy.wait()
        point_rows(sizes, values, slot, cell, amp, wave, aux)
    else:
        starts = [from_west[j] for j in range(sy // SUB)]
    place_point(tick, sizes, aux, south_hat)
    total = jnp.zeros((n_north, 2 * sz), F32)
    blocks = [spectrum_block(j, sizes, starts[j], values, aux, south_hat) for j in range(sy // SUB)]
    for j in range(sy // SUB):
        here = slice(j * SUB, (j + 1) * SUB)
        re, im = blocks[j]
        n = re.shape[0]
        spectrum[j, :n] = re
        spectrum[j, n:] = im
        high, low = split(jnp.concatenate([re, im], axis=1))
        east_table = tall[: 2 * n_east]
        start = 2 * n_east + 2 * n_north * j
        north_table = tall[start : start + 2 * n_north]
        main = dot(jnp.concatenate([east_table, north_table], axis=0), high)
        rest = dot(jnp.concatenate([east_table[:n_east], north_table[:n_north]], axis=0), low)
        part = main[:n_east] + main[n_east : 2 * n_east] + rest[:n_east]
        east_hat[:, here, :] = part.reshape(DEPTH, SUB, 2 * sz)
        at = 2 * n_east
        total += main[at : at + n_north] + main[at + n_north :] + rest[n_east:]

    zt = table("z")
    planes = [from_left(table("y"), east_hat[d]) for d in range(DEPTH)]
    lines = [p[:, :sz] for p in planes] + [p[:, sz:] for p in planes]
    lines = along_z(jnp.concatenate(lines, axis=0), zt).reshape(2, DEPTH, sy, sz)
    east[0], east[1] = correct(lines[0], lines[1], gain_east[0], gain_east[1])
    rows = from_left(table("south"), total)
    lines = along_z(jnp.concatenate([rows[:, :sz], rows[:, sz:]], axis=0), zt)
    north[0], north[1] = correct(lines[:n_north], lines[n_north:], gain_north[0], gain_north[1])


def west_kernel(sizes, places, narrow, west, _, out, west_hat):
    for j, block in enumerate(spread_west(sizes, table_of(narrow, places[0]), west, west_hat)):
        out[j] = block


def field_kernel(tick, sizes, places, *refs):
    sx, sy, sz = sizes
    refs = list(refs)
    take = lambda n: [refs.pop(0) for _ in range(n)]
    if tick == 0:
        narrow, spectrum, aux, region, vel, layers = take(6)
        field, gain_re, gain_im = take(3)
    else:
        narrow, spectrum, gain_re, gain_im = take(4)
        (field,) = take(1)
    (grid,) = take(1)
    table = table_of(narrow, places[0])
    for j in range(sy // SUB):
        invert_block(j, sizes, table, spectrum[j], grid)
    if tick == 0:
        gains = gains_of(sizes, layers, vel, wave_row(sizes, aux))
        columns = region[...].astype(F32).T
    for x in range(sx):
        raw = from_left(table("y"), grid[x])
        if tick == 0:
            g_re, g_im = gains(columns[:, x : x + 1], jnp.full((1, 1), float(x), F32), y_places(sizes))
            gain_re[x] = g_re
            gain_im[x] = g_im
        else:
            g_re, g_im = gain_re[x], gain_im[x]
        f_re, f_im = correct(raw[:, :sz], raw[:, sz:], g_re, g_im)
        field[0, x] = f_re.astype(BF16)
        field[1, x] = f_im.astype(BF16)


def last_kernel(tick, sizes, places, *refs):
    sx, sy, sz = sizes
    narrow, wide, aux, gain_re, gain_im, from_west, south = refs[:7]
    fields = refs[7 : 7 + tick]
    out, south_hat, grid, field, sems = refs[7 + tick :]
    copies = []
    for i, earlier in enumerate(fields):
        copy = pltpu.make_async_copy(earlier, out.at[i], sems.at[i])
        copy.start()
        copies.append(copy)
    table = table_of(narrow, places[0])
    values = values_of(wide, places[1])
    transform_south(sizes, table, south, south_hat)
    place_point(tick, sizes, aux, south_hat)
    blocks = [
        jnp.concatenate(spectrum_block(j, sizes, from_west[j], values, aux, south_hat), axis=0)
        for j in range(sy // SUB)
    ]
    for j in range(sy // SUB):
        invert_block(j, sizes, table, blocks[j], grid)
    for x in range(sx):
        raw = from_left(table("y"), grid[x])
        f_re, f_im = correct(raw[:, :sz], raw[:, sz:], gain_re[x], gain_im[x])
        field[0, x] = f_re.astype(BF16)
        field[1, x] = f_im.astype(BF16)
        if x % GROUP == GROUP - 1:
            span = pl.ds(x - GROUP + 1, GROUP)
            copy = pltpu.make_async_copy(field.at[:, span], out.at[tick, :, span], sems.at[len(copies)])
            copy.start()
            copies.append(copy)
    for copy in copies:
        copy.wait()


def call(kernel, name, args, out_shape, scratch, cost, in_specs=None, out_specs=None):
    vm = pl.BlockSpec(memory_space=pltpu.VMEM)
    return pl.pallas_call(
        kernel,
        out_shape=out_shape,
        in_specs=in_specs or [vm] * len(args),
        out_specs=out_specs or [vm] * len(out_shape),
        scratch_shapes=scratch,
        cost_estimate=pl.CostEstimate(flops=cost, bytes_accessed=4 << 20, transcendentals=0),
        compiler_params=pltpu.CompilerParams(vmem_limit_bytes=24 * 1024 * 1024),
        name=name,
    )(*args)


def local(west_in, south_in, region, pml_layers, vel_table, src_slot, src_cell, src_amp, wave_sq):
    sx, sy = region.shape
    sz = vel_table.shape[1]
    sizes = (sx, sy, sz)
    (narrow, narrow_at), (wide, wide_at), tall = constants(sx, sy, sz)
    places = (narrow_at, wide_at)
    shape = jax.ShapeDtypeStruct
    like = lambda a: shape(a.shape, a.dtype)
    vm = pl.BlockSpec(memory_space=pltpu.VMEM)
    west_hat = pltpu.VMEM((DEPTH, sy, 2 * sz), F32)
    south_hat = pltpu.VMEM((sx * (DEPTH + 1), 2 * sz), F32)
    hats = [south_hat, west_hat]
    west_shape = shape((sy // SUB, sx * SUB, 2 * sz), F32)
    grid = pltpu.VMEM((sx, sy, 2 * sz), F32)
    trace_shapes = [shape((2, DEPTH, sy, sz), F32), shape((2, sx * DEPTH, sz), F32)]
    spectrum_shape = shape((sy // SUB, 2 * sx * SUB, sz), F32)
    field_shape = shape((2, sx, sy, sz), BF16)
    gain_shapes = [shape((sx, sy, sz), F32)] * 2
    cost = 10**9

    south = south_in.reshape(2, sx * DEPTH, sz)
    tables = [jnp.asarray(t) for t in (narrow, wide, tall)]
    layers = pml_layers.reshape(1, 4)
    args = [tables[0], west_in, south, tables[1], src_slot, src_cell, src_amp, wave_sq.reshape(1, 1), tables[2]]
    args += [region, vel_table, layers]
    args = [pltpu.with_memory_space_constraint(a, pltpu.HBM) if a.size > 1 else a for a in args]
    moved = [west_in, south, src_slot, src_cell, src_amp, wave_sq.reshape(1, 1)]
    res = call(
        functools.partial(traces_kernel, 0, sizes, places),
        "traces0",
        args,
        trace_shapes
        + [spectrum_shape]
        + [like(t) for t in tables]
        + [shape((aux_rows(sizes), sz), F32)]
        + trace_shapes
        + [like(region), like(vel_table), like(layers)],
        hats + [west_hat] + [pltpu.VMEM(m.shape, m.dtype) for m in moved] + [pltpu.SemaphoreType.DMA((len(args),))],
        cost,
        in_specs=[pl.BlockSpec(memory_space=pltpu.HBM)] * len(args),
    )
    east, north, spectrum, narrow, wide, tall, aux, gain_east, gain_north, region, vel_table, layers = res
    fields = []
    gains = None
    for tick in range(1, TICKS):
        west = shift(east, "gx")
        south = shift(north, "gy")
        if tick == 1:
            given = [narrow, spectrum, aux, region, vel_table, layers]
            results = [field_shape, *gain_shapes]
        else:
            given = [narrow, spectrum, *gains]
            results = [field_shape]
        field, *made = call(
            functools.partial(field_kernel, tick - 1, sizes, places), f"field{tick - 1}", given, results, [grid], cost
        )
        gains = made or gains
        fields.append(field)
        (from_west,) = call(
            functools.partial(west_kernel, sizes, places),
            f"west{tick}",
            [narrow, west, field],
            [west_shape],
            [west_hat],
            cost,
            in_specs=[vm, vm, pl.BlockSpec(memory_space=pl.ANY)],
        )
        if tick + 1 < TICKS:
            east, north, spectrum = call(
                functools.partial(traces_kernel, tick, sizes, places),
                f"traces{tick}",
                [narrow, wide, tall, aux, gain_east, gain_north, from_west, south],
                trace_shapes + [spectrum_shape],
                hats,
                cost,
            )
    given = [narrow, wide, aux, *gains, from_west, south, *fields]
    (out,) = call(
        functools.partial(last_kernel, TICKS - 1, sizes, places),
        "last",
        given,
        [shape((TICKS, *field_shape.shape), BF16)],
        [south_hat, grid, pltpu.VMEM(field_shape.shape, BF16), pltpu.SemaphoreType.DMA((TICKS - 1 + sx // GROUP,))],
        cost,
        out_specs=[pl.BlockSpec(memory_space=pl.ANY)],
    )
    return out


def solution(mesh):
    in_specs = (
        P(None, "gx", "gy", None),
        P(None, "gx", "gy", None),
        P("gx", "gy"),
        P(None, "gx", "gy"),
        P(),
        P("gx", "gy"),
        P("gx", "gy"),
        P(),
        P(),
    )
    out_specs = P(None, None, "gx", "gy", None)
    return jax.shard_map(local, mesh=mesh, in_specs=in_specs, out_specs=out_specs, check_vma=False)
```

time: 48.3 us -> 42.5 us (0.88)
  waiting for transfers between devices: 12.6 us -> 5.69 us
  Pallas kernels: 18 us -> 19.1 us
    ppermute x4, waiting for transfers between devices: 12.6 us -> 5.69 us  [shift(): return lax.ppermute(array, axis, [(i, i + 1) for i in range(peers - 1)])]
    pallas_call x3 -> x7, Pallas kernels: 18 us -> 19.1 us  [call(): pl.pallas_call(kernel, out_shape=out_shape, in_specs=in_specs or [vm] * l...]
  transfers between devices with their start and end apart: 4 -> 4, of which waited for: 2 -> 2; matrix products, arithmetic and copies ran while one was open for 0% -> 0% of each run, Pallas kernels for 0% -> 16%
where the time goes in v1:
time: 42.5 us; the launch traced here: 42.3 us
  Pallas kernels  19.1 us (45%)
  starting transfers between devices  15.3 us (36%)
  waiting for transfers between devices  5.69 us (13%)
  between operations  2.18 us (5%)
    pallas_call x7, Pallas kernels, call(): pl.pallas_call(kernel, out_shape=out_shape, in_specs=in_specs or [vm] * l...  19.1 us
    ppermute x4, starting transfers between devices, shift(): return lax.ppermute(array, axis, [(i, i + 1) for i in range(peers - 1)])  15.3 us
    ppermute x4, waiting for transfers between devices, shift(): return lax.ppermute(array, axis, [(i, i + 1) for i in range(peers - 1)])  5.69 us
  transfers between devices with their start and end apart: 4, of which 2 were waited for; matrix products, arithmetic and copies ran while one was open for 0% of the time, Pallas kernels for 16%

profile of v1, /device:TPU:283, one launch (start us, length us, event | category | flops | bytes accessed | tf_op | source)
XLA Modules:
  0.0 42.3 jit_solution(304127409473168493)
XLA Ops:
  1.9 5.2 %traces0.1 = (f32[2,4,64,128]{3,2,1,0:T(8,128)S(1)}, f32[2,128,128]{2,1,0:T(8,128)S(1)}, f32[8,512,128]{2,1,0:T(8,128)S(1)}, bf16[1408,256]{1,0:T(8,128)(2,1)S(1...) custom-call(bf16[1408,256]{1,0:T(8,128)(2,1)} %constant.6.clone.refs, ...), custom_call_target="tpu_custom_call" | custom-call | flops 1000000000 | bytes 4194304 | tf_op jit(solution)/shard_map/traces0/pallas_call | solution.py:436
  7.2 4.9 %collective-permute-start = (f32[2,4,64,128]{3,2,1,0:T(8,128)S(1)}, f32[2,4,64,128]{3,2,1,0:T(8,128)S(1)}, u32[]{:S(2)}, u32[]{:S(2)}) collective-permute-start(f32[2,4,64,128]{3,2,1,0:T(8,128)S(1)} %get-tuple-element.35), channel_id=1, source_target_pairs={{0,16},{16,32},{32,48},{48,64},{64,80},{80,96},{96,112},{112,128},... | collective-permute-start | bytes 786440 | tf_op jit(solution)/shard_map/ppermute | solution.py:25
  12.1 4.0 %collective-permute-start.1 = (f32[2,128,128]{2,1,0:T(8,128)S(1)}, f32[2,128,128]{2,1,0:T(8,128)S(1)}, u32[]{:S(2)}, u32[]{:S(2)}) collective-permute-start(f32[2,128,128]{2,1,0:T(8,128)S(1)} %get-tuple-element.37), channel_id=1, source_target_pairs={{0,1},{1,2},{2,3},{3,4},{4,5},{5,6},{6,7},{7,8},{8,9},{9,10},{10,1... | collective-permute-start | bytes 393224 | tf_op jit(solution)/shard_map/ppermute | solution.py:25
  16.2 2.9 %field0.1 = (bf16[2,32,64,128]{3,2,1,0:T(8,128)(2,1)S(1)}, f32[32,64,128]{2,1,0:T(8,128)S(1)}, f32[32,64,128]{2,1,0:T(8,128)S(1)}) custom-call(bf16[1408,256]{1,0:T(8,128)(2,1)S(1)} %get-tuple-element.23.refs_0_.narrow, f32[8,512,128]{2,1,0:T(8,128)S(1)} %get-tuple-element.26.refs_1_, f32[104,128]{1,0:T(8,128)S(1)} %get-tuple-element.25.refs_2_.refs_3_, ...), custom_call_target="tpu_custom_call" | custom-call | flops 1000000000 | bytes 4194304 | tf_op jit(solution)/shard_map/field0/pallas_call | solution.py:436
  19.1 0.0 collective-permute-done.west
  19.1 0.9 %west1.1.refs_6_ = f32[8,256,256]{2,1,0:T(8,128)S(1)} custom-call(bf16[1408,256]{1,0:T(8,128)(2,1)S(1)} %get-tuple-element.23.refs_0_.narrow, f32[2,4,64,128]{3,2,1,0:T(8,128)S(1)} %collective-permute-done.west, bf16[2,32,64,128]{3,2,1,0:T(8,128)(2,1)S(1)} %get-tuple-element.36._.refs_7_), custom_call_target="tpu_custom_call" | custom-call | flops 1000000000 | bytes 4194304 | tf_op jit(solution)/shard_map/west1/pallas_call | solution.py:436
  20.0 1.5 %collective-permute-done.1.refs_7_ = f32[2,128,128]{2,1,0:T(8,128)S(1)} collective-permute-done((f32[2,128,128]{2,1,0:T(8,128)S(1)}, f32[2,128,128]{2,1,0:T(8,128)S(1)}, u32[]{:S(2)}, u32[]{:S(2)}) %collective-permute-start.1) | collective-permute-done | bytes 131104 | tf_op jit(solution)/shard_map/ppermute | solution.py:25
  21.5 2.8 %traces1.1 = (f32[2,4,64,128]{3,2,1,0:T(8,128)S(1)}, f32[2,128,128]{2,1,0:T(8,128)S(1)}, f32[8,512,128]{2,1,0:T(8,128)S(1)}) custom-call(bf16[1408,256]{1,0:T(8,128)(2,1)S(1)} %get-tuple-element.23.refs_0_.narrow, f32[544,128]{1,0:T(8,128)S(1)} %get-tuple-element.24.refs_1_, bf16[2112,256]{1,0:T(8,128)(2,1)S(1)} %get-tuple-element.32.refs_2_, ...), custom_call_target="tpu_custom_call" | custom-call | flops 1000000000 | bytes 4194304 | tf_op jit(solution)/shard_map/traces1/pallas_call | solution.py:436
  24.3 3.9 %collective-permute-start.2 = (f32[2,4,64,128]{3,2,1,0:T(8,128)S(1)}, f32[2,4,64,128]{3,2,1,0:T(8,128)S(1)}, u32[]{:S(2)}, u32[]{:S(2)}) collective-permute-start(f32[2,4,64,128]{3,2,1,0:T(8,128)S(1)} %get-tuple-element.38), channel_id=1, source_target_pairs={{0,16},{16,32},{32,48},{48,64},{64,80},{80,96},{96,112},{112,128},... | collective-permute-start | bytes 786440 | tf_op jit(solution)/shard_map/ppermute | solution.py:25
  28.2 2.4 %collective-permute-start.3 = (f32[2,128,128]{2,1,0:T(8,128)S(1)}, f32[2,128,128]{2,1,0:T(8,128)S(1)}, u32[]{:S(2)}, u32[]{:S(2)}) collective-permute-start(f32[2,128,128]{2,1,0:T(8,128)S(1)} %get-tuple-element.40), channel_id=1, source_target_pairs={{0,1},{1,2},{2,3},{3,4},{4,5},{5,6},{6,7},{7,8},{8,9},{9,10},{10,1... | collective-permute-start | bytes 393224 | tf_op jit(solution)/shard_map/ppermute | solution.py:25
  30.6 2.2 %field1.1._.refs_8_ = bf16[2,32,64,128]{3,2,1,0:T(8,128)(2,1)S(1)} custom-call(bf16[1408,256]{1,0:T(8,128)(2,1)S(1)} %get-tuple-element.23.refs_0_.narrow, f32[8,512,128]{2,1,0:T(8,128)S(1)} %get-tuple-element.39.refs_1_, f32[32,64,128]{2,1,0:T(8,128)S(1)} %get-tuple-element.30.refs_2_.refs_3_, f32[32,64,128]{2,1,0:T(8,128)S(1)} %get-tuple-element.31.refs_3_.refs_4_), custom_call_target="tpu_custom_call" | custom-call | flops 1000000000 | bytes 4194304 | tf_op jit(solution)/shard_map/field1/pallas_call | solution.py:436
  32.8 0.0 collective-permute-done.2.west
  32.8 0.9 %west2.1.refs_5_ = f32[8,256,256]{2,1,0:T(8,128)S(1)} custom-call(bf16[1408,256]{1,0:T(8,128)(2,1)S(1)} %get-tuple-element.23.refs_0_.narrow, f32[2,4,64,128]{3,2,1,0:T(8,128)S(1)} %collective-permute-done.2.west, bf16[2,32,64,128]{3,2,1,0:T(8,128)(2,1)S(1)} %field1.1._.refs_8_), custom_call_target="tpu_custom_call" | custom-call | flops 1000000000 | bytes 4194304 | tf_op jit(solution)/shard_map/west2/pallas_call | solution.py:436
  33.7 4.2 %collective-permute-done.3.refs_6_ = f32[2,128,128]{2,1,0:T(8,128)S(1)} collective-permute-done((f32[2,128,128]{2,1,0:T(8,128)S(1)}, f32[2,128,128]{2,1,0:T(8,128)S(1)}, u32[]{:S(2)}, u32[]{:S(2)}) %collective-permute-start.3) | collective-permute-done | bytes 131104 | tf_op jit(solution)/shard_map/ppermute | solution.py:25
  37.9 4.2 %last.1 = bf16[3,2,32,64,128]{4,3,2,1,0:T(8,128)(2,1)} custom-call(bf16[1408,256]{1,0:T(8,128)(2,1)S(1)} %get-tuple-element.23.refs_0_.narrow, f32[544,128]{1,0:T(8,128)S(1)} %get-tuple-element.24.refs_1_, f32[104,128]{1,0:T(8,128)S(1)} %get-tuple-element.25.refs_2_.refs_3_, f32[32,64,128]{2,1,0:T(8,128)S(1)} %get-tuple-element.30.refs_2_.refs_3_, ...), custom_call_target="tpu_custom_call" | custom-call | flops 1000000000 | bytes 4194304 | tf_op jit(solution)/shard_map/last/pallas_call | solution.py:436
Async XLA Ops:
  7.2 11.9 %collective-permute-start = (f32[2,4,64,128]{3,2,1,0:T(8,128)S(1)}, f32[2,4,64,128]{3,2,1,0:T(8,128)S(1)}, u32[]{:S(2)}, u32[]{:S(2)}) collective-permute-start(f32[2,4,64,128]{3,2,1,0:T(8,128)S(1)} %get-tuple-element.35), channel_id=1, source_target_pairs={{0,16},{16,32},{32,48},{48,64},{64,80},{80,96},{96,112},{112,128},... | collective-permute-start | bytes 786440 | tf_op jit(solution)/shard_map/ppermute | solution.py:25
  12.1 9.3 %collective-permute-start.1 = (f32[2,128,128]{2,1,0:T(8,128)S(1)}, f32[2,128,128]{2,1,0:T(8,128)S(1)}, u32[]{:S(2)}, u32[]{:S(2)}) collective-permute-start(f32[2,128,128]{2,1,0:T(8,128)S(1)} %get-tuple-element.37), channel_id=1, source_target_pairs={{0,1},{1,2},{2,3},{3,4},{4,5},{5,6},{6,7},{7,8},{8,9},{9,10},{10,1... | collective-permute-start | bytes 393224 | tf_op jit(solution)/shard_map/ppermute | solution.py:25
  24.3 8.5 %collective-permute-start.2 = (f32[2,4,64,128]{3,2,1,0:T(8,128)S(1)}, f32[2,4,64,128]{3,2,1,0:T(8,128)S(1)}, u32[]{:S(2)}, u32[]{:S(2)}) collective-permute-start(f32[2,4,64,128]{3,2,1,0:T(8,128)S(1)} %get-tuple-element.38), channel_id=1, source_target_pairs={{0,16},{16,32},{32,48},{48,64},{64,80},{80,96},{96,112},{112,128},... | collective-permute-start | bytes 786440 | tf_op jit(solution)/shard_map/ppermute | solution.py:25
  28.2 9.7 %collective-permute-start.3 = (f32[2,128,128]{2,1,0:T(8,128)S(1)}, f32[2,128,128]{2,1,0:T(8,128)S(1)}, u32[]{:S(2)}, u32[]{:S(2)}) collective-permute-start(f32[2,128,128]{2,1,0:T(8,128)S(1)} %get-tuple-element.40), channel_id=1, source_target_pairs={{0,1},{1,2},{2,3},{3,4},{4,5},{5,6},{6,7},{7,8},{8,9},{9,10},{10,1... | collective-permute-start | bytes 393224 | tf_op jit(solution)/shard_map/ppermute | solution.py:25

commit v2 on v1

--- a/solution.py
+++ b/solution.py
@@ -190,42 +190,54 @@
     south_hat[:n] = from_left(table("south"), jnp.concatenate([rows[0], rows[1]], axis=1))
 
 
-def place_point(tick, sizes, aux, south_hat):
+def place_point(tick, sizes, aux, point_hat):
     sx, sy, sz = sizes
     for c in range(2):
         row = sy + sx + 2 * tick + c
-        south_hat[DEPTH * sx :, c * sz : (c + 1) * sz] = aux[sy : sy + sx] * aux[row : row + 1]
-
-
-def spectrum_block(j, sizes, coeffs, values, aux, south_hat):
-    sx, sy, sz = sizes
-    here = slice(j * SUB, (j + 1) * SUB)
+        point_hat[:, c * sz : (c + 1) * sz] = aux[sy : sy + sx] * aux[row : row + 1]
+
+
+def inverse_symbol(j, sizes, values, aux):
+    sx, _, sz = sizes
     eigen_x = [float(v) for v in basis(sx)[1].astype(np.float32)]
     w2 = wave_row(sizes, aux)
     damping = jnp.broadcast_to(-DAMPING * w2, (SUB, sz))
     damping_square = damping * damping
     base = values("eigen", j * SUB, SUB) - w2
-    reach = [values("reach", d * sy + j * SUB, SUB) for d in range(DEPTH)] + [aux[here]]
+    pairs = []
+    for k in order(sx):
+        shifted = base + eigen_x[k]
+        size = shifted * shifted + damping_square
+        inverse = pl.reciprocal(size, approx=True)
+        inverse = inverse * (2.0 - size * inverse)
+        pairs.append((shifted * inverse, damping * inverse))
+    return pairs
+
+
+def spectrum_block(j, sizes, coeffs, values, pairs, south_hat, point=None):
+    sx, sy, sz = sizes
+    reach = [values("reach", d * sy + j * SUB, SUB) for d in range(DEPTH)]
+    if point is not None:
+        reach.append(point)
     new_re = []
     new_im = []
     for i, k in enumerate(order(sx)):
         line = slice(i * SUB, (i + 1) * SUB)
         c_re = coeffs[line, :sz]
         c_im = coeffs[line, sz:]
-        for d in range(DEPTH + 1):
+        for d, factor in enumerate(reach):
             row = k * DEPTH + d if d < DEPTH else sx * DEPTH + k
             row = slice(row, row + 1)
-            c_re += reach[d] * south_hat[row, :sz]
-            c_im += reach[d] * south_hat[row, sz:]
-        shifted = base + eigen_x[k]
-        size = shifted * shifted + damping_square
-        inverse = pl.reciprocal(size, approx=True)
-        inverse = inverse * (2.0 - size * inverse)
-        p = shifted * inverse
-        q = damping * inverse
+            c_re += factor * south_hat[row, :sz]
+            c_im += factor * south_hat[row, sz:]
+        p, q = pairs[i]
         new_re.append(c_re * p + c_im * q)
         new_im.append(c_im * p - c_re * q)
     return jnp.concatenate(new_re, axis=0), jnp.concatenate(new_im, axis=0)
+
+
+def kept_pairs(j, sizes, symbol):
+    return [tuple(symbol[c, j, i * SUB : (i + 1) * SUB] for c in range(2)) for i in range(sizes[0])]
 
 
 def invert_block(j, sizes, table, rows, grid):
@@ -303,7 +315,7 @@
         fetched = fetched[4:8] + fetched[9:] + fetched[:4] + fetched[8:9]
         east, north, spectrum, narrow, wide, tall, aux, gain_east, gain_north, region, vel, layers = take(12)
     else:
-        narrow, wide, tall, aux, gain_east, gain_north, from_west, south = take(8)
+        narrow, wide, tall, symbol, gain_east, gain_north, from_west, south = take(8)
         east, north, spectrum = take(3)
     south_hat, east_hat = take(2)
     if tick == 0:
@@ -330,11 +342,15 @@
         for copy in waits[10:]:
             copy.wait()
         point_rows(sizes, values, slot, cell, amp, wave, aux)
+        place_point(tick, sizes, aux, south_hat.at[DEPTH * sx :])
     else:
         starts = [from_west[j] for j in range(sy // SUB)]
-    place_point(tick, sizes, aux, south_hat)
     total = jnp.zeros((n_north, 2 * sz), F32)
-    blocks = [spectrum_block(j, sizes, starts[j], values, aux, south_hat) for j in range(sy // SUB)]
+    blocks = []
+    for j in range(sy // SUB):
+        pairs = inverse_symbol(j, sizes, values, aux) if tick == 0 else kept_pairs(j, sizes, symbol)
+        point = aux[j * SUB : (j + 1) * SUB] if tick == 0 else None
+        blocks.append(spectrum_block(j, sizes, starts[j], values, pairs, south_hat, point))
     for j in range(sy // SUB):
         here = slice(j * SUB, (j + 1) * SUB)
         re, im = blocks[j]
@@ -362,9 +378,15 @@
     north[0], north[1] = correct(lines[:n_north], lines[n_north:], gain_north[0], gain_north[1])
 
 
-def west_kernel(sizes, places, narrow, west, _, out, west_hat):
+def west_kernel(tick, sizes, places, narrow, aux, west, _, out, west_hat, point_hat):
+    sx, _, sz = sizes
+    place_point(tick, sizes, aux, point_hat)
     for j, block in enumerate(spread_west(sizes, table_of(narrow, places[0]), west, west_hat)):
-        out[j] = block
+        factor = aux[j * SUB : (j + 1) * SUB]
+        for i, k in enumerate(order(sx)):
+            line = slice(i * SUB, (i + 1) * SUB)
+            for part in (slice(0, sz), slice(sz, 2 * sz)):
+                out[j, line, part] = block[line, part] + factor * point_hat[k : k + 1, part]
 
 
 def field_kernel(tick, sizes, places, *refs):
@@ -372,8 +394,13 @@
     refs = list(refs)
     take = lambda n: [refs.pop(0) for _ in range(n)]
     if tick == 0:
-        narrow, spectrum, aux, region, vel, layers = take(6)
-        field, gain_re, gain_im = take(3)
+        narrow, spectrum, aux, region, vel, layers, wide = take(7)
+        field, gain_re, gain_im, symbol = take(4)
+        values = values_of(wide, places[1])
+        for j in range(sy // SUB):
+            for i, pair in enumerate(inverse_symbol(j, sizes, values, aux)):
+                for c in range(2):
+                    symbol[c, j, i * SUB : (i + 1) * SUB] = pair[c]
     else:
         narrow, spectrum, gain_re, gain_im = take(4)
         (field,) = take(1)
@@ -399,7 +426,7 @@
 
 def last_kernel(tick, sizes, places, *refs):
     sx, sy, sz = sizes
-    narrow, wide, aux, gain_re, gain_im, from_west, south = refs[:7]
+    narrow, wide, symbol, gain_re, gain_im, from_west, south = refs[:7]
     fields = refs[7 : 7 + tick]
     out, south_hat, grid, field, sems = refs[7 + tick :]
     copies = []
@@ -410,9 +437,8 @@
     table = table_of(narrow, places[0])
     values = values_of(wide, places[1])
     transform_south(sizes, table, south, south_hat)
-    place_point(tick, sizes, aux, south_hat)
     blocks = [
-        jnp.concatenate(spectrum_block(j, sizes, from_west[j], values, aux, south_hat), axis=0)
+        jnp.concatenate(spectrum_block(j, sizes, from_west[j], values, kept_pairs(j, sizes, symbol), south_hat), axis=0)
         for j in range(sy // SUB)
     ]
     for j in range(sy // SUB):
@@ -462,6 +488,7 @@
     trace_shapes = [shape((2, DEPTH, sy, sz), F32), shape((2, sx * DEPTH, sz), F32)]
     spectrum_shape = shape((sy // SUB, 2 * sx * SUB, sz), F32)
     field_shape = shape((2, sx, sy, sz), BF16)
+    symbol_shape = shape((2, sy // SUB, sx * SUB, sz), F32)
     gain_shapes = [shape((sx, sy, sz), F32)] * 2
     cost = 10**9
 
@@ -493,35 +520,36 @@
         west = shift(east, "gx")
         south = shift(north, "gy")
         if tick == 1:
-            given = [narrow, spectrum, aux, region, vel_table, layers]
-            results = [field_shape, *gain_shapes]
+            given = [narrow, spectrum, aux, region, vel_table, layers, wide]
+            results = [field_shape, *gain_shapes, symbol_shape]
         else:
             given = [narrow, spectrum, *gains]
             results = [field_shape]
         field, *made = call(
             functools.partial(field_kernel, tick - 1, sizes, places), f"field{tick - 1}", given, results, [grid], cost
         )
-        gains = made or gains
+        if made:
+            *gains, symbol = made
         fields.append(field)
         (from_west,) = call(
-            functools.partial(west_kernel, sizes, places),
+            functools.partial(west_kernel, tick, sizes, places),
             f"west{tick}",
-            [narrow, west, field],
+            [narrow, aux, west, field],
             [west_shape],
-            [west_hat],
+            [west_hat, pltpu.VMEM((sx, 2 * sz), F32)],
             cost,
-            in_specs=[vm, vm, pl.BlockSpec(memory_space=pl.ANY)],
+            in_specs=[vm, vm, vm, pl.BlockSpec(memory_space=pl.ANY)],
         )
         if tick + 1 < TICKS:
             east, north, spectrum = call(
                 functools.partial(traces_kernel, tick, sizes, places),
                 f"traces{tick}",
-                [narrow, wide, tall, aux, gain_east, gain_north, from_west, south],
+                [narrow, wide, tall, symbol, gain_east, gain_north, from_west, south],
                 trace_shapes + [spectrum_shape],
                 hats,
                 cost,
             )
-    given = [narrow, wide, aux, *gains, from_west, south, *fields]
+    given = [narrow, wide, symbol, *gains, from_west, south, *fields]
     (out,) = call(
         functools.partial(last_kernel, TICKS - 1, sizes, places),
         "last",

time: 42.5 us -> 41.4 us (0.974)
  Pallas kernels: 19.1 us -> 18.1 us
    pallas_call x7, Pallas kernels: 19.1 us -> 18.1 us  [call(): pl.pallas_call(kernel, out_shape=out_shape, in_specs=in_specs or [vm] * l...]
  transfers between devices with their start and end apart: 4 -> 4, of which waited for: 2 -> 2; matrix products, arithmetic and copies ran while one was open for 0% -> 0% of each run, Pallas kernels for 16% -> 17%
where the time goes in v2:
time: 41.4 us; the launch traced here: 41.1 us
  Pallas kernels  18.1 us (44%)
  starting transfers between devices  15.3 us (37%)
  waiting for transfers between devices  5.6 us (14%)
  between operations  2.19 us (5%)
    pallas_call x7, Pallas kernels, call(): pl.pallas_call(kernel, out_shape=out_shape, in_specs=in_specs or [vm] * l...  18.1 us
    ppermute x4, starting transfers between devices, shift(): return lax.ppermute(array, axis, [(i, i + 1) for i in range(peers - 1)])  15.3 us
    ppermute x4, waiting for transfers between devices, shift(): return lax.ppermute(array, axis, [(i, i + 1) for i in range(peers - 1)])  5.6 us
  transfers between devices with their start and end apart: 4, of which 2 were waited for; matrix products, arithmetic and copies ran while one was open for 0% of the time, Pallas kernels for 17%

profile of v2, /device:TPU:283, one launch (start us, length us, event | category | flops | bytes accessed | tf_op | source)
XLA Modules:
  0.0 41.1 jit_solution(16679177800888208237)
XLA Ops:
  1.9 5.2 %traces0.1 = (f32[2,4,64,128]{3,2,1,0:T(8,128)S(1)}, f32[2,128,128]{2,1,0:T(8,128)S(1)}, f32[8,512,128]{2,1,0:T(8,128)S(1)}, bf16[1408,256]{1,0:T(8,128)(2,1)S(1...) custom-call(bf16[1408,256]{1,0:T(8,128)(2,1)} %constant.6.clone.refs, ...), custom_call_target="tpu_custom_call" | custom-call | flops 1000000000 | bytes 4194304 | tf_op jit(solution)/shard_map/traces0/pallas_call | solution.py:462
  7.1 4.9 %collective-permute-start = (f32[2,4,64,128]{3,2,1,0:T(8,128)S(1)}, f32[2,4,64,128]{3,2,1,0:T(8,128)S(1)}, u32[]{:S(2)}, u32[]{:S(2)}) collective-permute-start(f32[2,4,64,128]{3,2,1,0:T(8,128)S(1)} %get-tuple-element.37), channel_id=1, source_target_pairs={{0,16},{16,32},{32,48},{48,64},{64,80},{80,96},{96,112},{112,128},... | collective-permute-start | bytes 786440 | tf_op jit(solution)/shard_map/ppermute | solution.py:25
  12.1 4.0 %collective-permute-start.1 = (f32[2,128,128]{2,1,0:T(8,128)S(1)}, f32[2,128,128]{2,1,0:T(8,128)S(1)}, u32[]{:S(2)}, u32[]{:S(2)}) collective-permute-start(f32[2,128,128]{2,1,0:T(8,128)S(1)} %get-tuple-element.39), channel_id=1, source_target_pairs={{0,1},{1,2},{2,3},{3,4},{4,5},{5,6},{6,7},{7,8},{8,9},{9,10},{10,1... | collective-permute-start | bytes 393224 | tf_op jit(solution)/shard_map/ppermute | solution.py:25
  16.1 3.0 %field0.1 = (bf16[2,32,64,128]{3,2,1,0:T(8,128)(2,1)S(1)}, f32[32,64,128]{2,1,0:T(8,128)S(1)}, f32[32,64,128]{2,1,0:T(8,128)S(1)}, f32[2,8,256,128]{3,2,1,0:T(8,128)S(1)}) custom-call(bf16[1408,256]{1,0:T(8,128)(2,1)S(1)} %get-tuple-element.24.refs_0_.narrow, f32[8,512,128]{2,1,0:T(8,128)S(1)} %get-tuple-element.26.refs_1_, ...), custom_call_target="tpu_custom_call" | custom-call | flops 1000000000 | bytes 4194304 | tf_op jit(solution)/shard_map/field0/pallas_call | solution.py:462
  19.1 0.0 collective-permute-done.west
  19.2 0.9 %west1.1.refs_6_ = f32[8,256,256]{2,1,0:T(8,128)S(1)} custom-call(bf16[1408,256]{1,0:T(8,128)(2,1)S(1)} %get-tuple-element.24.refs_0_.narrow, f32[104,128]{1,0:T(8,128)S(1)} %get-tuple-element.27.refs_2_.aux, f32[2,4,64,128]{3,2,1,0:T(8,128)S(1)} %collective-permute-done.west, bf16[2,32,64,128]{3,2,1,0:T(8,128)(2,1)S(1)} %get-tuple-element.38._.refs_7_), custom_call_target="tpu_custom_call" | custom-call | flops 1000000000 | bytes 4194304 | tf_op jit(solution)/shard_map/west1/pallas_call | solution.py:462
  20.1 1.3 %collective-permute-done.1.refs_7_ = f32[2,128,128]{2,1,0:T(8,128)S(1)} collective-permute-done((f32[2,128,128]{2,1,0:T(8,128)S(1)}, f32[2,128,128]{2,1,0:T(8,128)S(1)}, u32[]{:S(2)}, u32[]{:S(2)}) %collective-permute-start.1) | collective-permute-done | bytes 131104 | tf_op jit(solution)/shard_map/ppermute | solution.py:25
  21.4 2.3 %traces1.1 = (f32[2,4,64,128]{3,2,1,0:T(8,128)S(1)}, f32[2,128,128]{2,1,0:T(8,128)S(1)}, f32[8,512,128]{2,1,0:T(8,128)S(1)}) custom-call(bf16[1408,256]{1,0:T(8,128)(2,1)S(1)} %get-tuple-element.24.refs_0_.narrow, f32[544,128]{1,0:T(8,128)S(1)} %get-tuple-element.25.refs_6_.refs_1_, bf16[2112,256]{1,0:T(8,128)(2,1)S(1)} %get-tuple-element.34.refs_2_, ...), custom_call_target="tpu_custom_call" | custom-call | flops 1000000000 | bytes 4194304 | tf_op jit(solution)/shard_map/traces1/pallas_call | solution.py:462
  23.8 3.9 %collective-permute-start.2 = (f32[2,4,64,128]{3,2,1,0:T(8,128)S(1)}, f32[2,4,64,128]{3,2,1,0:T(8,128)S(1)}, u32[]{:S(2)}, u32[]{:S(2)}) collective-permute-start(f32[2,4,64,128]{3,2,1,0:T(8,128)S(1)} %get-tuple-element.40), channel_id=1, source_target_pairs={{0,16},{16,32},{32,48},{48,64},{64,80},{80,96},{96,112},{112,128},... | collective-permute-start | bytes 786440 | tf_op jit(solution)/shard_map/ppermute | solution.py:25
  27.7 2.4 %collective-permute-start.3 = (f32[2,128,128]{2,1,0:T(8,128)S(1)}, f32[2,128,128]{2,1,0:T(8,128)S(1)}, u32[]{:S(2)}, u32[]{:S(2)}) collective-permute-start(f32[2,128,128]{2,1,0:T(8,128)S(1)} %get-tuple-element.42), channel_id=1, source_target_pairs={{0,1},{1,2},{2,3},{3,4},{4,5},{5,6},{6,7},{7,8},{8,9},{9,10},{10,1... | collective-permute-start | bytes 393224 | tf_op jit(solution)/shard_map/ppermute | solution.py:25
  30.0 2.2 %field1.1._.refs_8_ = bf16[2,32,64,128]{3,2,1,0:T(8,128)(2,1)S(1)} custom-call(bf16[1408,256]{1,0:T(8,128)(2,1)S(1)} %get-tuple-element.24.refs_0_.narrow, f32[8,512,128]{2,1,0:T(8,128)S(1)} %get-tuple-element.41.refs_1_, f32[32,64,128]{2,1,0:T(8,128)S(1)} %get-tuple-element.32.refs_2_.refs_3_, f32[32,64,128]{2,1,0:T(8,128)S(1)} %get-tuple-element.33.refs_3_.refs_4_), custom_call_target="tpu_custom_call" | custom-call | flops 1000000000 | bytes 4194304 | tf_op jit(solution)/shard_map/field1/pallas_call | solution.py:462
  32.2 0.0 collective-permute-done.2.west
  32.2 0.9 %west2.1.refs_5_ = f32[8,256,256]{2,1,0:T(8,128)S(1)} custom-call(bf16[1408,256]{1,0:T(8,128)(2,1)S(1)} %get-tuple-element.24.refs_0_.narrow, f32[104,128]{1,0:T(8,128)S(1)} %get-tuple-element.27.refs_2_.aux, f32[2,4,64,128]{3,2,1,0:T(8,128)S(1)} %collective-permute-done.2.west, bf16[2,32,64,128]{3,2,1,0:T(8,128)(2,1)S(1)} %field1.1._.refs_8_), custom_call_target="tpu_custom_call" | custom-call | flops 1000000000 | bytes 4194304 | tf_op jit(solution)/shard_map/west2/pallas_call | solution.py:462
  33.1 4.3 %collective-permute-done.3.refs_6_ = f32[2,128,128]{2,1,0:T(8,128)S(1)} collective-permute-done((f32[2,128,128]{2,1,0:T(8,128)S(1)}, f32[2,128,128]{2,1,0:T(8,128)S(1)}, u32[]{:S(2)}, u32[]{:S(2)}) %collective-permute-start.3) | collective-permute-done | bytes 131104 | tf_op jit(solution)/shard_map/ppermute | solution.py:25
  37.4 3.6 %last.1 = bf16[3,2,32,64,128]{4,3,2,1,0:T(8,128)(2,1)} custom-call(bf16[1408,256]{1,0:T(8,128)(2,1)S(1)} %get-tuple-element.24.refs_0_.narrow, f32[544,128]{1,0:T(8,128)S(1)} %get-tuple-element.25.refs_6_.refs_1_, f32[2,8,256,128]{3,2,1,0:T(8,128)S(1)} %get-tuple-element.31.refs_3_.refs_2_, f32[32,64,128]{2,1,0:T(8,128)S(1)} %get-tuple-element.32.refs_2_.refs_3_, ...), custom_call_target="tpu_custom_call" | custom-call | flops 1000000000 | bytes 4194304 | tf_op jit(solution)/shard_map/last/pallas_call | solution.py:462
Async XLA Ops:
  7.1 12.0 %collective-permute-start = (f32[2,4,64,128]{3,2,1,0:T(8,128)S(1)}, f32[2,4,64,128]{3,2,1,0:T(8,128)S(1)}, u32[]{:S(2)}, u32[]{:S(2)}) collective-permute-start(f32[2,4,64,128]{3,2,1,0:T(8,128)S(1)} %get-tuple-element.37), channel_id=1, source_target_pairs={{0,16},{16,32},{32,48},{48,64},{64,80},{80,96},{96,112},{112,128},... | collective-permute-start | bytes 786440 | tf_op jit(solution)/shard_map/ppermute | solution.py:25
  12.1 9.3 %collective-permute-start.1 = (f32[2,128,128]{2,1,0:T(8,128)S(1)}, f32[2,128,128]{2,1,0:T(8,128)S(1)}, u32[]{:S(2)}, u32[]{:S(2)}) collective-permute-start(f32[2,128,128]{2,1,0:T(8,128)S(1)} %get-tuple-element.39), channel_id=1, source_target_pairs={{0,1},{1,2},{2,3},{3,4},{4,5},{5,6},{6,7},{7,8},{8,9},{9,10},{10,1... | collective-permute-start | bytes 393224 | tf_op jit(solution)/shard_map/ppermute | solution.py:25
  23.8 8.4 %collective-permute-start.2 = (f32[2,4,64,128]{3,2,1,0:T(8,128)S(1)}, f32[2,4,64,128]{3,2,1,0:T(8,128)S(1)}, u32[]{:S(2)}, u32[]{:S(2)}) collective-permute-start(f32[2,4,64,128]{3,2,1,0:T(8,128)S(1)} %get-tuple-element.40), channel_id=1, source_target_pairs={{0,16},{16,32},{32,48},{48,64},{64,80},{80,96},{96,112},{112,128},... | collective-permute-start | bytes 786440 | tf_op jit(solution)/shard_map/ppermute | solution.py:25
  27.7 9.7 %collective-permute-start.3 = (f32[2,128,128]{2,1,0:T(8,128)S(1)}, f32[2,128,128]{2,1,0:T(8,128)S(1)}, u32[]{:S(2)}, u32[]{:S(2)}) collective-permute-start(f32[2,128,128]{2,1,0:T(8,128)S(1)} %get-tuple-element.42), channel_id=1, source_target_pairs={{0,1},{1,2},{2,3},{3,4},{4,5},{5,6},{6,7},{7,8},{8,9},{9,10},{10,1... | collective-permute-start | bytes 393224 | tf_op jit(solution)/shard_map/ppermute | solution.py:25

commit v3 on v2

--- a/solution.py
+++ b/solution.py
@@ -12,7 +12,7 @@
 DEPTH = 4
 TICKS = 3
 SUB = 8
-GROUP = 4
+GROUP = 8
 DAMPING = 0.25
 PEAK = 4.0
 BASE = 6.0
@@ -326,15 +326,12 @@
             copy = pltpu.make_async_copy(fetched[i], target, fetch_sems.at[i])
             copy.start()
             waits.append(copy)
-        for copy in waits[:7]:
-            copy.wait()
     table = table_of(narrow, places[0])
     values = values_of(wide, places[1])
     n_east = DEPTH * SUB
     n_north = DEPTH * sx
     if tick == 0:
-        trace_gains(sizes, region, vel, layers, wave, gain_east, gain_north)
-        for copy in waits[7:10]:
+        for copy in waits[:10]:
             copy.wait()
         starts = spread_west(sizes, table, west, west_hat)
     transform_south(sizes, table, south, south_hat)
@@ -368,6 +365,8 @@
         at = 2 * n_east
         total += main[at : at + n_north] + main[at + n_north :] + rest[n_east:]
 
+    if tick == 0:
+        trace_gains(sizes, region, vel, layers, wave, gain_east, gain_north)
     zt = table("z")
     planes = [from_left(table("y"), east_hat[d]) for d in range(DEPTH)]
     lines = [p[:, :sz] for p in planes] + [p[:, sz:] for p in planes]

time: 41.4 us -> 41.3 us (level)
  no operation moved by 1% of the time
where the time goes in v3:
time: 41.3 us; the launch traced here: 41.1 us
  Pallas kernels  18 us (44%)
  starting transfers between devices  15.3 us (37%)
  waiting for transfers between devices  5.59 us (14%)
  between operations  2.19 us (5%)
    pallas_call x7, Pallas kernels, call(): pl.pallas_call(kernel, out_shape=out_shape, in_specs=in_specs or [vm] * l...  18 us
    ppermute x4, starting transfers between devices, shift(): return lax.ppermute(array, axis, [(i, i + 1) for i in range(peers - 1)])  15.3 us
    ppermute x4, waiting for transfers between devices, shift(): return lax.ppermute(array, axis, [(i, i + 1) for i in range(peers - 1)])  5.59 us
  transfers between devices with their start and end apart: 4, of which 2 were waited for; matrix products, arithmetic and copies ran while one was open for 0% of the time, Pallas kernels for 17%

profile of v3, /device:TPU:283, one launch (start us, length us, event | category | flops | bytes accessed | tf_op | source)
XLA Modules:
  0.0 41.1 jit_solution(987512260540534102)
XLA Ops:
  1.9 5.1 %traces0.1 = (f32[2,4,64,128]{3,2,1,0:T(8,128)S(1)}, f32[2,128,128]{2,1,0:T(8,128)S(1)}, f32[8,512,128]{2,1,0:T(8,128)S(1)}, bf16[1408,256]{1,0:T(8,128)(2,1)S(1...) custom-call(bf16[1408,256]{1,0:T(8,128)(2,1)} %constant.6.clone.refs, ...), custom_call_target="tpu_custom_call" | custom-call | flops 1000000000 | bytes 4194304 | tf_op jit(solution)/shard_map/traces0/pallas_call | solution.py:461
  7.1 4.9 %collective-permute-start = (f32[2,4,64,128]{3,2,1,0:T(8,128)S(1)}, f32[2,4,64,128]{3,2,1,0:T(8,128)S(1)}, u32[]{:S(2)}, u32[]{:S(2)}) collective-permute-start(f32[2,4,64,128]{3,2,1,0:T(8,128)S(1)} %get-tuple-element.37), channel_id=1, source_target_pairs={{0,16},{16,32},{32,48},{48,64},{64,80},{80,96},{96,112},{112,128},... | collective-permute-start | bytes 786440 | tf_op jit(solution)/shard_map/ppermute | solution.py:25
  12.0 4.1 %collective-permute-start.1 = (f32[2,128,128]{2,1,0:T(8,128)S(1)}, f32[2,128,128]{2,1,0:T(8,128)S(1)}, u32[]{:S(2)}, u32[]{:S(2)}) collective-permute-start(f32[2,128,128]{2,1,0:T(8,128)S(1)} %get-tuple-element.39), channel_id=1, source_target_pairs={{0,1},{1,2},{2,3},{3,4},{4,5},{5,6},{6,7},{7,8},{8,9},{9,10},{10,1... | collective-permute-start | bytes 393224 | tf_op jit(solution)/shard_map/ppermute | solution.py:25
  16.1 3.0 %field0.1 = (bf16[2,32,64,128]{3,2,1,0:T(8,128)(2,1)S(1)}, f32[32,64,128]{2,1,0:T(8,128)S(1)}, f32[32,64,128]{2,1,0:T(8,128)S(1)}, f32[2,8,256,128]{3,2,1,0:T(8,128)S(1)}) custom-call(bf16[1408,256]{1,0:T(8,128)(2,1)S(1)} %get-tuple-element.24.refs_0_.narrow, f32[8,512,128]{2,1,0:T(8,128)S(1)} %get-tuple-element.26.refs_1_, ...), custom_call_target="tpu_custom_call" | custom-call | flops 1000000000 | bytes 4194304 | tf_op jit(solution)/shard_map/field0/pallas_call | solution.py:461
  19.1 0.0 collective-permute-done.west
  19.1 0.9 %west1.1.refs_6_ = f32[8,256,256]{2,1,0:T(8,128)S(1)} custom-call(bf16[1408,256]{1,0:T(8,128)(2,1)S(1)} %get-tuple-element.24.refs_0_.narrow, f32[104,128]{1,0:T(8,128)S(1)} %get-tuple-element.27.refs_2_.aux, f32[2,4,64,128]{3,2,1,0:T(8,128)S(1)} %collective-permute-done.west, bf16[2,32,64,128]{3,2,1,0:T(8,128)(2,1)S(1)} %get-tuple-element.38._.refs_7_), custom_call_target="tpu_custom_call" | custom-call | flops 1000000000 | bytes 4194304 | tf_op jit(solution)/shard_map/west1/pallas_call | solution.py:461
  20.0 1.3 %collective-permute-done.1.refs_7_ = f32[2,128,128]{2,1,0:T(8,128)S(1)} collective-permute-done((f32[2,128,128]{2,1,0:T(8,128)S(1)}, f32[2,128,128]{2,1,0:T(8,128)S(1)}, u32[]{:S(2)}, u32[]{:S(2)}) %collective-permute-start.1) | collective-permute-done | bytes 131104 | tf_op jit(solution)/shard_map/ppermute | solution.py:25
  21.4 2.3 %traces1.1 = (f32[2,4,64,128]{3,2,1,0:T(8,128)S(1)}, f32[2,128,128]{2,1,0:T(8,128)S(1)}, f32[8,512,128]{2,1,0:T(8,128)S(1)}) custom-call(bf16[1408,256]{1,0:T(8,128)(2,1)S(1)} %get-tuple-element.24.refs_0_.narrow, f32[544,128]{1,0:T(8,128)S(1)} %get-tuple-element.25.refs_6_.refs_1_, bf16[2112,256]{1,0:T(8,128)(2,1)S(1)} %get-tuple-element.34.refs_2_, ...), custom_call_target="tpu_custom_call" | custom-call | flops 1000000000 | bytes 4194304 | tf_op jit(solution)/shard_map/traces1/pallas_call | solution.py:461
  23.7 3.9 %collective-permute-start.2 = (f32[2,4,64,128]{3,2,1,0:T(8,128)S(1)}, f32[2,4,64,128]{3,2,1,0:T(8,128)S(1)}, u32[]{:S(2)}, u32[]{:S(2)}) collective-permute-start(f32[2,4,64,128]{3,2,1,0:T(8,128)S(1)} %get-tuple-element.40), channel_id=1, source_target_pairs={{0,16},{16,32},{32,48},{48,64},{64,80},{80,96},{96,112},{112,128},... | collective-permute-start | bytes 786440 | tf_op jit(solution)/shard_map/ppermute | solution.py:25
  27.6 2.4 %collective-permute-start.3 = (f32[2,128,128]{2,1,0:T(8,128)S(1)}, f32[2,128,128]{2,1,0:T(8,128)S(1)}, u32[]{:S(2)}, u32[]{:S(2)}) collective-permute-start(f32[2,128,128]{2,1,0:T(8,128)S(1)} %get-tuple-element.42), channel_id=1, source_target_pairs={{0,1},{1,2},{2,3},{3,4},{4,5},{5,6},{6,7},{7,8},{8,9},{9,10},{10,1... | collective-permute-start | bytes 393224 | tf_op jit(solution)/shard_map/ppermute | solution.py:25
  30.0 2.2 %field1.1._.refs_8_ = bf16[2,32,64,128]{3,2,1,0:T(8,128)(2,1)S(1)} custom-call(bf16[1408,256]{1,0:T(8,128)(2,1)S(1)} %get-tuple-element.24.refs_0_.narrow, f32[8,512,128]{2,1,0:T(8,128)S(1)} %get-tuple-element.41.refs_1_, f32[32,64,128]{2,1,0:T(8,128)S(1)} %get-tuple-element.32.refs_2_.refs_3_, f32[32,64,128]{2,1,0:T(8,128)S(1)} %get-tuple-element.33.refs_3_.refs_4_), custom_call_target="tpu_custom_call" | custom-call | flops 1000000000 | bytes 4194304 | tf_op jit(solution)/shard_map/field1/pallas_call | solution.py:461
  32.1 0.0 collective-permute-done.2.west
  32.2 0.9 %west2.1.refs_5_ = f32[8,256,256]{2,1,0:T(8,128)S(1)} custom-call(bf16[1408,256]{1,0:T(8,128)(2,1)S(1)} %get-tuple-element.24.refs_0_.narrow, f32[104,128]{1,0:T(8,128)S(1)} %get-tuple-element.27.refs_2_.aux, f32[2,4,64,128]{3,2,1,0:T(8,128)S(1)} %collective-permute-done.2.west, bf16[2,32,64,128]{3,2,1,0:T(8,128)(2,1)S(1)} %field1.1._.refs_8_), custom_call_target="tpu_custom_call" | custom-call | flops 1000000000 | bytes 4194304 | tf_op jit(solution)/shard_map/west2/pallas_call | solution.py:461
  33.1 4.2 %collective-permute-done.3.refs_6_ = f32[2,128,128]{2,1,0:T(8,128)S(1)} collective-permute-done((f32[2,128,128]{2,1,0:T(8,128)S(1)}, f32[2,128,128]{2,1,0:T(8,128)S(1)}, u32[]{:S(2)}, u32[]{:S(2)}) %collective-permute-start.3) | collective-permute-done | bytes 131104 | tf_op jit(solution)/shard_map/ppermute | solution.py:25
  37.3 3.6 %last.1 = bf16[3,2,32,64,128]{4,3,2,1,0:T(8,128)(2,1)} custom-call(bf16[1408,256]{1,0:T(8,128)(2,1)S(1)} %get-tuple-element.24.refs_0_.narrow, f32[544,128]{1,0:T(8,128)S(1)} %get-tuple-element.25.refs_6_.refs_1_, f32[2,8,256,128]{3,2,1,0:T(8,128)S(1)} %get-tuple-element.31.refs_3_.refs_2_, f32[32,64,128]{2,1,0:T(8,128)S(1)} %get-tuple-element.32.refs_2_.refs_3_, ...), custom_call_target="tpu_custom_call" | custom-call | flops 1000000000 | bytes 4194304 | tf_op jit(solution)/shard_map/last/pallas_call | solution.py:461
Async XLA Ops:
  7.1 12.0 %collective-permute-start = (f32[2,4,64,128]{3,2,1,0:T(8,128)S(1)}, f32[2,4,64,128]{3,2,1,0:T(8,128)S(1)}, u32[]{:S(2)}, u32[]{:S(2)}) collective-permute-start(f32[2,4,64,128]{3,2,1,0:T(8,128)S(1)} %get-tuple-element.37), channel_id=1, source_target_pairs={{0,16},{16,32},{32,48},{48,64},{64,80},{80,96},{96,112},{112,128},... | collective-permute-start | bytes 786440 | tf_op jit(solution)/shard_map/ppermute | solution.py:25
  12.0 9.3 %collective-permute-start.1 = (f32[2,128,128]{2,1,0:T(8,128)S(1)}, f32[2,128,128]{2,1,0:T(8,128)S(1)}, u32[]{:S(2)}, u32[]{:S(2)}) collective-permute-start(f32[2,128,128]{2,1,0:T(8,128)S(1)} %get-tuple-element.39), channel_id=1, source_target_pairs={{0,1},{1,2},{2,3},{3,4},{4,5},{5,6},{6,7},{7,8},{8,9},{9,10},{10,1... | collective-permute-start | bytes 393224 | tf_op jit(solution)/shard_map/ppermute | solution.py:25
  23.7 8.5 %collective-permute-start.2 = (f32[2,4,64,128]{3,2,1,0:T(8,128)S(1)}, f32[2,4,64,128]{3,2,1,0:T(8,128)S(1)}, u32[]{:S(2)}, u32[]{:S(2)}) collective-permute-start(f32[2,4,64,128]{3,2,1,0:T(8,128)S(1)} %get-tuple-element.40), channel_id=1, source_target_pairs={{0,16},{16,32},{32,48},{48,64},{64,80},{80,96},{96,112},{112,128},... | collective-permute-start | bytes 786440 | tf_op jit(solution)/shard_map/ppermute | solution.py:25
  27.6 9.7 %collective-permute-start.3 = (f32[2,128,128]{2,1,0:T(8,128)S(1)}, f32[2,128,128]{2,1,0:T(8,128)S(1)}, u32[]{:S(2)}, u32[]{:S(2)}) collective-permute-start(f32[2,128,128]{2,1,0:T(8,128)S(1)} %get-tuple-element.42), channel_id=1, source_target_pairs={{0,1},{1,2},{2,3},{3,4},{4,5},{5,6},{6,7},{7,8},{8,9},{9,10},{10,1... | collective-permute-start | bytes 393224 | tf_op jit(solution)/shard_map/ppermute | solution.py:25
